TPU v7x, 32 devices: a whole 2x2x4 slice. The times are simulated.
32 devices in a mesh: dom: 16 (over z, y, x), sub: 2 (over core).
Axes of the slice: x: 2, y: 2, z: 4, core: 2. Of those that a mesh axis runs over, the one named last changes fastest.
Arguments:
- a_blocks: bfloat16 [2048, 8, 128, 128], P(('dom', 'sub')), may hold values from -6 to 6
- nbr_offset: int32 [2048, 8], P(('dom', 'sub')), may hold values from -3 to 3
- nbr_count: int32 [2048], P(('dom', 'sub')), may hold values from 4 to 8
- prolong: bfloat16 [2048, 128, 128], P(('dom', 'sub')), may hold values from -0.5 to 0.5
- owner_start: int32 [32], replicated, may hold values from 0 to 2047, as said below
Outputs:
- coarse: float32 [512, 7, 128, 128], P(('dom', 'sub'))
Inputs may be any that keep to these rules, and one draw needn't show every extreme that they name: owner_start[0] = 0, owner_start[1] = 112, and owner_start[d] - d * 64 lies in 0 to 48 for every d.
All inputs are finite; a program needn't handle non-finite values.
Results may differ from a plain program's by a relative error of at most 0.0029.
Values may be sent and summed in bfloat16 or wider, within the bound.
No kernel may reach another device: no remote copies, remote signals or barrier semaphores. Data moves between devices by JAX's collectives and lax.ppermute only.
A program may use at most 256 MiB of HBM per device.

v0:
```python
import functools

import jax
import jax.numpy as jnp
from jax import lax
from jax.experimental import pallas as pl
from jax.experimental.pallas import tpu as pltpu
from jax.sharding import PartitionSpec as P

W = 3
KC = 7
AD = 16
SMAX = 48
NQ = 2
UNROLL = 6
HALF = 22
AXES = ("dom", "sub")


AHEAD = 16
SHIFT = 20
FAR = 1024

T_AGG = 0
T_OFF = 128
T_BASE = 192
T_ROW = 256
T_DST = 384
T_CUM = 512
T_COLUMN = 640
T_N = 448
T_H = 449
T_LO = 450
T_HI = 451
T_S = 452
T_OWN0 = 453
T_OWN1 = 454
T_OWN2 = 455
T_LAST = 456
T_NEXT = 457
T_GROUP = 128
T_LEN = 768


def starts(pos, devices, rows, own_ref):
    def start(owner):
        at = jnp.clip(owner, 0, devices - 1)
        given = jnp.where(owner < devices, own_ref[at], devices * rows)
        return jnp.where(owner < 0, 0, given) - pos * rows

    return [start(pos + step) for step in (-1, 0, 1, 2)]


def row_start(begin, length, agg):
    return begin + lax.shift_right_logical(agg * length + (AD - 1), 4)


def scan_rows(pos, devices, rows, begins, table):
    total = devices * rows
    first = pos * rows
    scale = []
    for owner in range(3):
        length = jnp.maximum(begins[owner + 1] - begins[owner], 1)
        scale.append(lax.div(length + (2**SHIFT - 1), length) * AD)
    items = jnp.int32(0)
    aggs = []
    for at in range(rows + 2 * W):
        row = at - W

        def local(owner):
            return lax.shift_right_logical((row - begins[owner]) * scale[owner], SHIFT) + owner * AD

        if row >= rows:
            agg = jnp.where(row >= begins[2], local(2), local(1))
            agg = jnp.where(first + row < total, agg, aggs[-1])
            column = jnp.where(first + row < total, agg, FAR)
        elif row >= SMAX:
            agg = column = local(1)
        elif row >= 0:
            agg = column = jnp.where(row >= begins[1], local(1), local(0))
        else:
            agg = jnp.where(first > 0, local(0), AD)
            column = jnp.where(first > 0, agg, FAR)
        aggs.append(agg)
        table[T_AGG + at] = agg
        table[T_COLUMN + at] = column
        if at >= 2 * W:
            table[T_CUM + at - 2 * W] = items
            items = items + (lax.shift_right_logical(agg - aggs[at - 2 * W], 1) + 1)
    table[T_CUM + rows] = items


def scan_sent(rows, begins, table, places):
    count = begins[1]
    length = begins[1] - begins[0]
    sent = table[T_CUM + count]
    share = jnp.maximum(lax.div(table[T_CUM + rows], 3), lax.div(7 * sent, 16))
    lowest = jnp.where(count > 0, table[T_AGG + W], AD)

    def span(agg):
        return (
            jnp.maximum(row_start(begins[0], length, agg), 0),
            jnp.minimum(row_start(begins[0], length, agg + 1), count),
        )

    def step(agg, carry):
        end, floor, even = carry
        row, stop = span(agg)
        off = end - table[T_AGG + row]
        table[T_OFF + agg] = off
        table[T_BASE + agg] = end
        table[T_ROW + agg] = row
        begin = end
        end = off + table[T_AGG + stop - 1 + 2 * W] + 1
        if places:

            def put(slot, carry):
                table[T_DST + slot] = (KC - 1) * agg + W + slot - off
                return carry

            lax.fori_loop(begin, end, put, 0)
        floor = jnp.where(row < W, end, floor)
        even = jnp.where(sent - table[T_CUM + row] > share, end, even)
        return end, floor, even

    end, floor, even = lax.fori_loop(lowest, AD, step, (0, 0, 0))
    split = jnp.maximum(jnp.maximum(end - HALF, floor), jnp.minimum(even, HALF))
    table[T_N] = end
    table[T_H] = split
    if places:
        return

    def find(agg, carry):
        low, high = carry
        base = table[T_BASE + agg]
        row, stop = span(agg)
        low = jnp.where(base <= split, row, low)
        high = jnp.where(base < split, stop, high)
        return low, high

    low, high = lax.fori_loop(lowest, AD, find, (0, 0))
    table[T_LO] = jnp.where(split >= end, count, low)
    table[T_HI] = high


def share_own(rows, begins, table):
    count = begins[1]
    length = begins[2] - begins[1]
    whole = table[T_CUM + rows]
    first = jnp.maximum(lax.div(whole, 3) - table[T_CUM + count] + table[T_CUM + table[T_LO]], 0)
    second = jnp.maximum(lax.div(3 * whole, 8) - table[T_CUM + table[T_HI]], 0)

    def step(agg, carry):
        own0, own1, own2 = carry
        row = row_start(count, length, agg)
        fresh = (row >= W) & (own0 < 0)
        own0 = jnp.where(fresh, row, own0)
        own1 = jnp.where(fresh, row, own1)
        own2 = jnp.where(fresh, row, own2)
        inside = (own0 >= 0) & (row <= rows - W)
        done = table[T_CUM + row]
        own1 = jnp.where(inside & (done <= table[T_CUM + jnp.maximum(own0, 0)] + first), row, own1)
        own2 = jnp.where(inside & (done <= table[T_CUM + jnp.maximum(own1, 0)] + second), row, own2)
        return own0, own1, own2

    own0, own1, own2 = lax.fori_loop(0, AD, step, (-1, -1, -1))
    table[T_OWN0] = own0
    table[T_OWN1] = own1
    table[T_OWN2] = own2
    table[T_S] = count
    table[T_LAST] = table[T_AGG + rows - 1 + W] - AD


def apply_row(row, group, nbr, cnt, table, blocks, window, applied):
    right = []
    left = []
    slots = cnt[row]
    lowest = table[T_AGG + row] + NQ * group
    for k in range(blocks.shape[1]):
        at = row + W + nbr[k, row]
        near = window[at]
        column = jnp.where(k < slots, table[T_COLUMN + at], FAR) - lowest
        zero = jnp.zeros_like(near)
        right.append(jnp.concatenate([jnp.where(column == q, near, zero) for q in range(NQ)], axis=1))
        left.append(blocks[row, k])
    applied[...] = jnp.dot(
        jnp.concatenate(left, axis=1), jnp.concatenate(right, axis=0), preferred_element_type=jnp.float32
    ).astype(applied.dtype)


def all_rows(ranges, down, ahead, low_slot, high_slot, nbr, cnt, table, blocks, window, applied, turned, items, row_sems, a_hbm, acc, writes):
    (lo0, hi0), (lo1, hi1) = ranges
    width = window.shape[2]
    count = table[T_S]
    turn = hi0 - lo0

    def row_at(index):
        sent = hi0 - 1 - index if down else lo0 + index
        return jnp.where(index < turn, sent, lo1 + index - turn)

    def start(index, amount):
        row = row_at(index)

        @pl.when((row < ahead) | (row >= count))
        def _():
            pltpu.make_async_copy(a_hbm.at[row], blocks.at[row], row_sems.at[row]).start()

        for group in range((2 * W) // NQ + 1):
            items[amount + group] = row + T_GROUP * group
        return amount + table[T_CUM + row + 1] - table[T_CUM + row]

    amount = lax.fori_loop(0, turn + hi1 - lo1, start, 0)

    def item(index):
        at = items[jnp.clip(index, 0, amount - 1)]
        valid = (index >= 0) & (index < amount)
        return at & (T_GROUP - 1), lax.shift_right_logical(at, 7), valid

    def add(row, group, valid, u):
        term = jnp.dot(turned[u][...], applied[u][...], preferred_element_type=jnp.float32)
        agg = table[T_AGG + row + W]
        highest = table[T_AGG + row + 2 * W]
        own = row >= count
        for q in range(NQ):
            target = table[T_AGG + row] + NQ * group + q
            sent = table[T_OFF + agg] + target
            kept = (KC - 1) * agg - KC * AD + W + target
            ok = valid & (target <= highest) & (own | ((sent >= low_slot) & (sent < high_slot)))
            at = jnp.where(ok, jnp.where(own, HALF + 1 + kept, sent - low_slot), HALF)
            acc[at] += term[:, q * width : (q + 1) * width]

    def add_block(begin):
        for u in range(UNROLL):
            row, group, valid = item(begin + u)
            add(row, group, valid, u)

    def block(step, written):
        begin = step * UNROLL
        row, _, valid = item(begin - UNROLL)
        whole = jnp.where(valid, jnp.clip(table[T_AGG + row + W] - AD, 0, AD), 0)
        writes.start(written, whole)
        for u in range(UNROLL):
            row, group, valid = item(begin + u)

            @pl.when(valid & (group == 0))
            def _():
                pltpu.make_async_copy(a_hbm.at[row], blocks.at[row], row_sems.at[row]).wait()

        add_block(begin - UNROLL)
        for u in range(UNROLL):
            row, group, valid = item(begin + u)
            apply_row(row, group, nbr, cnt, table, blocks, window, applied[u])
            turned[u][...] = window[row + W].T
        return jnp.maximum(written, whole)

    def run():
        @pl.when(amount > 0)
        def _():
            steps = lax.div(amount + UNROLL - 1, UNROLL)
            written = lax.fori_loop(0, steps, block, jnp.int32(0))
            add_block((steps - 1) * UNROLL)
            writes.start(written, AD)

    return run


def clear(acc, begin, end):
    def step(at, carry):
        acc[at] = jnp.zeros(acc.shape[1:], acc.dtype)
        return carry

    lax.fori_loop(begin, end, step, 0)


def give(acc, out):
    def step(at, carry):
        out[at] = acc[at].astype(out.dtype)
        return carry

    lax.fori_loop(0, HALF, step, 0)


class Writes:
    def __init__(self, ranges, acc, coarse, sems):
        self.ranges, self.acc, self.coarse, self.sems = ranges, acc, coarse, sems

    def each(self, begin, end, act):
        def step(agg, carry):
            inside = False
            for low, high in self.ranges:
                inside = inside | ((agg >= low) & (agg < high))

            @pl.when(inside)
            def _():
                act(
                    pltpu.make_async_copy(
                        self.acc.at[pl.ds(HALF + 1 + agg * KC, KC)],
                        self.coarse.at[pl.ds(agg * KC, KC)],
                        self.sems.at[agg],
                    )
                )

            return carry

        lax.fori_loop(begin, end, step, 0)

    def start(self, begin, end):
        self.each(begin, end, lambda copy: copy.start())

    def wait(self):
        self.each(0, AD, lambda copy: copy.wait())


def position():
    place = 0
    for axis in AXES:
        place = place * lax.axis_size(axis) + lax.axis_index(axis)
    return place


def late_kernel(
    devices, own_hbm, nbr_hbm, cnt_hbm, a_hbm, p_hbm, out, tail, coarse, table, own, nbr, cnt, blocks, window, applied, turned, items, acc, sems, row_sems, out_sems
):
    rows = a_hbm.shape[0]
    pos = position()
    copies = [
        pltpu.make_async_copy(own_hbm, own, sems.at[0]),
        pltpu.make_async_copy(nbr_hbm, nbr, sems.at[1]),
        pltpu.make_async_copy(cnt_hbm, cnt, sems.at[2]),
        pltpu.make_async_copy(p_hbm, window.at[pl.ds(W, rows)], sems.at[3]),
    ]
    for copy in copies:
        copy.start()
    copies[0].wait()
    begins = starts(pos, devices, rows, own)
    for at, begin in enumerate(starts(pos + 1, devices, rows, own)):
        table[T_NEXT + at] = begin
    count = begins[1]
    ahead = jnp.maximum(count - AHEAD, W)

    def fetch(row):
        return pltpu.make_async_copy(a_hbm.at[row], blocks.at[row], row_sems.at[row])

    def prefetch(index, carry):
        fetch(count - 1 - index).start()
        return carry

    def drain(row, carry):
        fetch(row).wait()
        return carry

    lax.fori_loop(0, count - ahead, prefetch, 0)
    scan_rows(pos, devices, rows, begins, table)
    scan_sent(rows, begins, table, False)
    share_own(rows, begins, table)
    low, own0, own1 = table[T_LO], table[T_OWN0], table[T_OWN1]
    begin = table[T_AGG + own0 + W] - AD
    stop = table[T_AGG + own1 + W] - AD
    writes = Writes([(begin, stop)], acc, coarse, out_sems)
    run = all_rows(
        ((low, count), (own0, own1)), True, ahead, table[T_H], table[T_N], nbr, cnt, table, blocks, window, applied, turned, items, row_sems, a_hbm, acc, writes
    )
    clear(acc, 0, HALF)
    clear(acc, HALF + 1 + begin * KC, HALF + 1 + stop * KC)
    copies[1].wait()
    copies[2].wait()
    copies[3].wait()
    for at in range(W):
        out[HALF + at] = window[W + at]
        tail[at] = window[rows + at]
    run()
    give(acc, out)
    lax.fori_loop(ahead, low, drain, 0)
    writes.wait()


def early_kernel(
    devices, table, nbr_hbm, cnt_hbm, a_hbm, p_hbm, before, _, out, coarse, nbr, cnt, blocks, window, applied, turned, items, acc, sems, row_sems, out_sems
):
    rows = a_hbm.shape[0]
    pos = position()
    own1, own2 = table[T_OWN1], table[T_OWN2]
    copies = [
        pltpu.make_async_copy(p_hbm, window.at[pl.ds(W, rows)], sems.at[0]),
        pltpu.make_async_copy(before, window.at[pl.ds(0, W)], sems.at[1]),
        pltpu.make_async_copy(nbr_hbm, nbr, sems.at[2]),
        pltpu.make_async_copy(cnt_hbm, cnt, sems.at[3]),
    ]
    for copy in copies:
        copy.start()
    begin = table[T_AGG + own1 + W] - AD
    stop = table[T_AGG + own2 + W] - AD
    writes = Writes([(begin, stop)], acc, coarse, out_sems)
    run = all_rows(
        ((0, table[T_HI]), (own1, own2)), False, table[T_S], 0, table[T_H], nbr, cnt, table, blocks, window, applied, turned, items, row_sems, a_hbm, acc, writes
    )
    clear(acc, 0, HALF)
    clear(acc, HALF + 1 + begin * KC, HALF + 1 + stop * KC)
    copies[2].wait()
    copies[3].wait()
    copies[0].wait()
    copies[1].wait()
    run()
    give(acc, out)
    writes.wait()


def own_kernel(
    devices, table, nbr_hbm, cnt_hbm, a_hbm, p_hbm, before, got, _, coarse, edge, merge, nbr, cnt, blocks, window, applied, turned, items, acc, sems, row_sems, out_sems
):
    rows = a_hbm.shape[0]
    pos = position()
    count, own0, own2, last = table[T_S], table[T_OWN0], table[T_OWN2], table[T_LAST]
    copies = [
        pltpu.make_async_copy(p_hbm, window.at[pl.ds(W, rows)], sems.at[0]),
        pltpu.make_async_copy(before, window.at[pl.ds(0, W)], sems.at[1]),
        pltpu.make_async_copy(nbr_hbm, nbr, sems.at[2]),
        pltpu.make_async_copy(cnt_hbm, cnt, sems.at[3]),
    ]
    for copy in copies:
        copy.start()
    skip = table[T_AGG + own0 + W] - AD
    resume = table[T_AGG + own2 + W] - AD
    writes = Writes([(0, skip), (resume, last + 1)], acc, coarse, out_sems)
    others = Writes([(last + 1, AD)], acc, coarse, out_sems)
    run = all_rows(
        ((count, own0), (own2, rows)), False, count, 0, 0, nbr, cnt, table, blocks, window, applied, turned, items, row_sems, a_hbm, acc, writes
    )
    clear(acc, HALF + 1, HALF + 1 + skip * KC)
    clear(acc, HALF + 1 + resume * KC, HALF + 1 + AD * KC)
    merge[T_N] = 0
    merge[T_H] = 0

    @pl.when(pos + 1 < devices)
    def _():
        begins = [table[T_NEXT + at] for at in range(4)]
        scan_rows(pos + 1, devices, rows, begins, merge)
        scan_sent(rows, begins, merge, True)

    split = merge[T_H]

    def add(slot, carry):
        acc[HALF + 1 + merge[T_DST + slot]] += got[slot - split].astype(jnp.float32)
        return carry

    lax.fori_loop(split, merge[T_N], add, 0)
    others.start(last + 1, AD)
    for at in range(W):
        window[W + rows + at] = got[HALF + at]
    copies[2].wait()
    copies[3].wait()
    copies[0].wait()
    copies[1].wait()
    run()
    for at in range(KC):
        edge[at] = acc[HALF + 1 + last * KC + at]
    merge[T_LAST] = last
    writes.wait()
    others.wait()


def merge_kernel(merge, got, edge, _, coarse, held, sems):
    last = merge[T_LAST] * KC

    def store(slot):
        return pltpu.make_async_copy(held.at[slot], coarse.at[merge[T_DST + slot]], sems.at[slot])

    def start(slot, carry):
        at = merge[T_DST + slot] - last
        base = edge[jnp.minimum(at, KC - 1)]
        held[slot] = got[slot].astype(jnp.float32) + jnp.where(at < KC, base, jnp.zeros_like(base))
        store(slot).start()
        return carry

    def wait(slot, carry):
        store(slot).wait()
        return carry

    lax.fori_loop(0, merge[T_H], start, 0)
    lax.fori_loop(0, merge[T_H], wait, 0)


SMEM = pl.BlockSpec(memory_space=pltpu.SMEM)
VMEM = pl.BlockSpec(memory_space=pltpu.VMEM)
HBM = pl.BlockSpec(memory_space=pltpu.HBM)
DMA = pltpu.SemaphoreType.DMA


def params(size=58):
    return pltpu.CompilerParams(vmem_limit_bytes=size * 1024 * 1024)


def cost(flops, moved):
    return pl.CostEstimate(flops=flops, bytes_accessed=moved, transcendentals=0)


def passed(block, step):
    devices = range(lax.axis_size(AXES))
    return lax.ppermute(block, AXES, [(i, i + step) for i in devices if i + step in devices])


def shards(a_blocks, nbr_offset, nbr_count, prolong, owner_start):
    devices = lax.axis_size(AXES)
    rows, slots, size, width = a_blocks.shape
    flops = rows * slots * size * size * width * 2
    moved = rows * slots * size * width * 2
    work = [
        pltpu.SMEM(nbr_offset.shape[::-1], jnp.int32),
        pltpu.SMEM(nbr_count.shape, jnp.int32),
        pltpu.VMEM((rows, slots, size, size), jnp.bfloat16),
        pltpu.VMEM((rows + 2 * W, size, width), jnp.bfloat16),
        [pltpu.VMEM((size, NQ * width), jnp.bfloat16)] * UNROLL,
        [pltpu.VMEM((width, size), jnp.bfloat16)] * UNROLL,
        pltpu.SMEM(((2 * W // NQ + 1) * (rows + 1),), jnp.int32),
        pltpu.VMEM((HALF + 1 + AD * KC, width, width), jnp.float32),
        DMA((4,)),
        DMA((rows,)),
        DMA((AD,)),
    ]
    table_shape = jax.ShapeDtypeStruct((T_LEN,), jnp.int32)
    coarse_shape = jax.ShapeDtypeStruct((AD * KC, width, width), jnp.float32)
    offsets = nbr_offset.T

    late, tail, coarse, table = pl.pallas_call(
        functools.partial(late_kernel, devices),
        out_shape=(
            jax.ShapeDtypeStruct((HALF + W, width, width), jnp.bfloat16),
            jax.ShapeDtypeStruct((W, size, width), jnp.bfloat16),
            coarse_shape,
            table_shape,
        ),
        in_specs=[HBM] * 5,
        out_specs=(VMEM, VMEM, HBM, SMEM),
        scratch_shapes=[pltpu.SMEM(owner_start.shape, jnp.int32)] + work,
        compiler_params=params(),
        cost_estimate=cost(flops // 3, moved // 3),
        name="late_rows",
    )(owner_start, offsets, nbr_count, a_blocks, prolong)
    before = passed(tail, 1)
    got_late = passed(late, -1)
    early, coarse = pl.pallas_call(
        functools.partial(early_kernel, devices),
        out_shape=(jax.ShapeDtypeStruct((HALF, width, width), jnp.bfloat16), coarse_shape),
        in_specs=[SMEM] + [HBM] * 6,
        out_specs=(VMEM, HBM),
        scratch_shapes=work,
        input_output_aliases={6: 1},
        compiler_params=params(50),
        cost_estimate=cost(flops // 3, moved // 3),
        name="early_rows",
    )(table, offsets, nbr_count, a_blocks, prolong, before, coarse)
    got_early = passed(early, -1)
    coarse, edge, merge = pl.pallas_call(
        functools.partial(own_kernel, devices),
        out_shape=(coarse_shape, jax.ShapeDtypeStruct((KC, width, width), jnp.float32), table_shape),
        in_specs=[SMEM] + [HBM] * 5 + [VMEM, HBM],
        out_specs=(HBM, VMEM, SMEM),
        scratch_shapes=work,
        input_output_aliases={7: 0},
        compiler_params=params(50),
        cost_estimate=cost(flops // 3, moved // 3),
        name="own_rows",
    )(table, offsets, nbr_count, a_blocks, prolong, before, got_late, coarse)
    coarse = pl.pallas_call(
        merge_kernel,
        out_shape=coarse_shape,
        in_specs=[SMEM, VMEM, VMEM, HBM],
        out_specs=HBM,
        scratch_shapes=[pltpu.VMEM((HALF, width, width), jnp.float32), DMA((HALF,))],
        input_output_aliases={3: 0},
        compiler_params=params(32),
        name="merge_rows",
    )(merge, got_early, edge, coarse)
    return coarse.reshape(AD, KC, width, width)


def solution(mesh):
    placed = (
        P(("dom", "sub"), None, None, None),
        P(("dom", "sub"), None),
        P(("dom", "sub")),
        P(("dom", "sub"), None, None),
        P(),
    )
    return jax.shard_map(
        shards,
        mesh=mesh,
        in_specs=placed,
        out_specs=P(("dom", "sub"), None, None, None),
        check_vma=False,
    )
```

profile of v0, /device:TPU:25, one launch (start us, length us, event | category | flops | bytes accessed | tf_op | source)
XLA Modules:
  0.0 43.2 jit_solution(7402861171348028518)
XLA Ops:
  0.0 0.0 copy-start
  0.0 0.0 copy-start.1
  0.0 0.0 copy-start.3
  0.0 10.2 %late_rows.1 = (bf16[25,128,128]{2,1,0:T(8,128)(2,1)}, bf16[3,128,128]{2,1,0:T(8,128)(2,1)}, f32[112,128,128]{2,1,0:T(8,128)}, s32[768]{0:T(1024)}) custom-call(s32[32]{0:T(128)} %own_hbm.1, s32[8,64]{1,0:T(8,128)} %bitcast.2, s32[64]{0:T(128)} %cnt_hbm.5, bf16[64,8,128,128]{3,2,1,0:T(8,128)(2,1)} %a_hbm.5, bf16[64,128,128]{2,1,0:T(8,128)(2,1)} %p_hbm.5), custom_call_target="tpu_custom_call" | custom-call | flops 715827904 | bytes 5592405 | tf_op jit(solution)/shard_map/late_rows/pallas_call | solution.py:524
  10.2 2.7 %collective-permute-start = (bf16[3,128,128]{2,1,0:T(8,128)(2,1)}, bf16[3,128,128]{2,1,0:T(8,128)(2,1)S(1)}, u32[]{:S(2)}, u32[]{:S(2)}) collective-permute-start(bf16[3,128,128]{2,1,0:T(8,128)(2,1)} %get-tuple-element.15), channel_id=1, source_target_pairs={{0,1},{1,2},{2,3},{3,4},{4,5},{5,6},{6,7},{7,8},{8,9},{9,10},{10,1... | collective-permute-start | bytes 294920 | tf_op jit(solution)/shard_map/ppermute | solution.py:499
  12.9 1.9 %collective-permute-start.1 = (bf16[25,128,128]{2,1,0:T(8,128)(2,1)}, bf16[25,128,128]{2,1,0:T(8,128)(2,1)S(1)}, u32[]{:S(2)}, u32[]{:S(2)}) collective-permute-start(bf16[25,128,128]{2,1,0:T(8,128)(2,1)} %get-tuple-element.16), channel_id=1, source_target_pairs={{1,0},{2,1},{3,2},{4,3},{5,4},{6,5},{7,6},{8,7},{9,8},{10,9},{11,1... | collective-permute-start | bytes 2457608 | tf_op jit(solution)/shard_map/ppermute | solution.py:499
  14.8 0.0 collective-permute-done.before
  14.9 0.0 copy-done
  14.9 0.0 copy-done.1
  14.9 0.0 copy-done.3
  14.9 0.0 copy-start.2
  14.9 0.7 %copy-done.2 = s32[768]{0:T(1024)S(1)} copy-done((s32[768]{0:T(1024)S(1)}, s32[768]{0:T(1024)}, u32[]{:S(2)}) %copy-start.2) | copy-done | bytes 3096
  15.6 9.0 %early_rows.1 = (bf16[22,128,128]{2,1,0:T(8,128)(2,1)S(1)}, f32[112,128,128]{2,1,0:T(8,128)}) custom-call(s32[768]{0:T(1024)S(1)} %copy-done.2, s32[8,64]{1,0:T(8,128)S(1)} %bitcast.3, s32[64]{0:T(128)S(1)} %copy-done.3, bf16[64,8,128,128]{3,2,1,0:T(8,128)(2,1)} %a_hbm.5, bf16[64,128,128]{2,1,0:T(8,128)(2,1)S(1)} %copy-done, ...), custom_call_target="tpu_custom_call", output_to_operand_aliasing={{1}: (6, {})} | custom-call | flops 715827904 | bytes 5592405 | tf_op jit(solution)/shard_map/early_rows/pallas_call | solution.py:541
  24.5 5.5 %collective-permute-start.2 = (bf16[22,128,128]{2,1,0:T(8,128)(2,1)S(1)}, bf16[22,128,128]{2,1,0:T(8,128)(2,1)S(1)}, u32[]{:S(2)}, u32[]{:S(2)}) collective-permute-start(bf16[22,128,128]{2,1,0:T(8,128)(2,1)S(1)} %get-tuple-element.20), channel_id=1, source_target_pairs={{1,0},{2,1},{3,2},{4,3},{5,4},{6,5},{7,6},{8,7},{9,8},{10,9},{11,1... | collective-permute-start | bytes 2162696 | tf_op jit(solution)/shard_map/ppermute | solution.py:499
  30.1 0.0 collective-permute-done.1.got
  30.1 11.5 %own_rows.1 = (f32[112,128,128]{2,1,0:T(8,128)}, f32[7,128,128]{2,1,0:T(8,128)S(1)}, s32[768]{0:T(1024)S(1)}) custom-call(s32[768]{0:T(1024)S(1)} %copy-done.2, s32[8,64]{1,0:T(8,128)S(1)} %bitcast.4, s32[64]{0:T(128)S(1)} %copy-done.3, bf16[64,8,128,128]{3,2,1,0:T(8,128)(2,1)} %a_hbm.5, ...), custom_call_target="tpu_custom_call", output_to_operand_aliasing={{0}: (7, {})} | custom-call | flops 715827904 | bytes 5592405 | tf_op jit(solution)/shard_map/own_rows/pallas_call | solution.py:553
  41.6 0.0 collective-permute-done.2.got
  41.6 1.7 %merge_rows.1 = f32[112,128,128]{2,1,0:T(8,128)} custom-call(s32[768]{0:T(1024)S(1)} %get-tuple-element.19.merge, bf16[22,128,128]{2,1,0:T(8,128)(2,1)S(1)} %collective-permute-done.2.got, f32[7,128,128]{2,1,0:T(8,128)S(1)} %get-tuple-element.21.edge, f32[112,128,128]{2,1,0:T(8,128)} %get-tuple-element.22._), custom_call_target="tpu_custom_call", output_to_operand_aliasing={{}: (3, {})} | custom-call | tf_op jit(solution)/shard_map/merge_rows/pallas_call | solution.py:564
Async XLA Ops:
  0.0 14.9 %copy-start = (bf16[64,128,128]{2,1,0:T(8,128)(2,1)S(1)}, bf16[64,128,128]{2,1,0:T(8,128)(2,1)}, u32[]{:S(2)}) copy-start(bf16[64,128,128]{2,1,0:T(8,128)(2,1)} %p_hbm.5) | copy-start | bytes 6291460
  0.0 14.9 %copy-start.1 = (s32[64,8]{0,1:T(8,128)S(1)}, s32[64,8]{0,1:T(8,128)}, u32[]{:S(2)}) copy-start(s32[64,8]{0,1:T(8,128)} %param.6) | copy-start | bytes 6148
  0.0 14.9 %copy-start.3 = (s32[64]{0:T(128)S(1)}, s32[64]{0:T(128)}, u32[]{:S(2)}) copy-start(s32[64]{0:T(128)} %cnt_hbm.5) | copy-start | bytes 772
  10.2 4.7 %collective-permute-start = (bf16[3,128,128]{2,1,0:T(8,128)(2,1)}, bf16[3,128,128]{2,1,0:T(8,128)(2,1)S(1)}, u32[]{:S(2)}, u32[]{:S(2)}) collective-permute-start(bf16[3,128,128]{2,1,0:T(8,128)(2,1)} %get-tuple-element.15), channel_id=1, source_target_pairs={{0,1},{1,2},{2,3},{3,4},{4,5},{5,6},{6,7},{7,8},{8,9},{9,10},{10,1... | collective-permute-start | bytes 294920 | tf_op jit(solution)/shard_map/ppermute | solution.py:499
  12.9 17.2 %collective-permute-start.1 = (bf16[25,128,128]{2,1,0:T(8,128)(2,1)}, bf16[25,128,128]{2,1,0:T(8,128)(2,1)S(1)}, u32[]{:S(2)}, u32[]{:S(2)}) collective-permute-start(bf16[25,128,128]{2,1,0:T(8,128)(2,1)} %get-tuple-element.16), channel_id=1, source_target_pairs={{1,0},{2,1},{3,2},{4,3},{5,4},{6,5},{7,6},{8,7},{9,8},{10,9},{11,1... | collective-permute-start | bytes 2457608 | tf_op jit(solution)/shard_map/ppermute | solution.py:499
  14.9 0.7 %copy-start.2 = (s32[768]{0:T(1024)S(1)}, s32[768]{0:T(1024)}, u32[]{:S(2)}) copy-start(s32[768]{0:T(1024)} %get-tuple-element.14.table) | copy-start | bytes 9220
  24.5 17.0 %collective-permute-start.2 = (bf16[22,128,128]{2,1,0:T(8,128)(2,1)S(1)}, bf16[22,128,128]{2,1,0:T(8,128)(2,1)S(1)}, u32[]{:S(2)}, u32[]{:S(2)}) collective-permute-start(bf16[22,128,128]{2,1,0:T(8,128)(2,1)S(1)} %get-tuple-element.20), channel_id=1, source_target_pairs={{1,0},{2,1},{3,2},{4,3},{5,4},{6,5},{7,6},{8,7},{9,8},{10,9},{11,1... | collective-permute-start | bytes 2162696 | tf_op jit(solution)/shard_map/ppermute | solution.py:499
where the time goes:
time: 43.5 us; the launch traced here: 43.2 us
  Pallas kernels  32.3 us (74%)
  starting transfers between devices  10.2 us (23%)
  local copies, waits for them, and re-layouts  0.68 us (2%)
    pallas_call x1, Pallas kernels, shards(): pl.pallas_call(functools.partial(own_kernel, devices), out_shape=(coarse_...  11.5 us
    pallas_call x1, Pallas kernels, shards(): pl.pallas_call(functools.partial(late_kernel, devices), out_shape=(jax.Sh...  10.2 us
    ppermute x3, starting transfers between devices, passed(): lax.ppermute(block, AXES, [(i, i + step) for i in devices if i + step in...  10.2 us
    pallas_call x1, Pallas kernels, shards(): pl.pallas_call(functools.partial(early_kernel, devices), out_shape=(jax.S...  8.98 us
    pallas_call x1, Pallas kernels, shards(): pl.pallas_call(merge_kernel, out_shape=coarse_shape, in_specs=[SMEM, VMEM...  1.66 us
  transfers between devices with their start and end apart: 3, of which 0 were waited for; matrix products, arithmetic and copies ran while one was open for 0% of the time, Pallas kernels for 47%

commit v1 on v0

--- a/solution.py
+++ b/solution.py
@@ -13,7 +13,8 @@
 SMAX = 48
 NQ = 2
 UNROLL = 6
-HALF = 22
+HALF = 25
+EARLY = 18
 AXES = ("dom", "sub")
 
 
@@ -55,7 +56,7 @@
     return begin + lax.shift_right_logical(agg * length + (AD - 1), 4)
 
 
-def scan_rows(pos, devices, rows, begins, table):
+def scan_rows(pos, devices, rows, begins, table, upto):
     total = devices * rows
     first = pos * rows
     scale = []
@@ -64,7 +65,7 @@
         scale.append(lax.div(length + (2**SHIFT - 1), length) * AD)
     items = jnp.int32(0)
     aggs = []
-    for at in range(rows + 2 * W):
+    for at in range(upto + 2 * W):
         row = at - W
 
         def local(owner):
@@ -83,18 +84,19 @@
             column = jnp.where(first > 0, agg, FAR)
         aggs.append(agg)
         table[T_AGG + at] = agg
-        table[T_COLUMN + at] = column
+        if upto == rows:
+            table[T_COLUMN + at] = column
         if at >= 2 * W:
             table[T_CUM + at - 2 * W] = items
             items = items + (lax.shift_right_logical(agg - aggs[at - 2 * W], 1) + 1)
-    table[T_CUM + rows] = items
-
-
-def scan_sent(rows, begins, table, places):
+    table[T_CUM + upto] = items
+
+
+def scan_sent(begins, table, places):
     count = begins[1]
     length = begins[1] - begins[0]
     sent = table[T_CUM + count]
-    share = jnp.maximum(lax.div(table[T_CUM + rows], 3), lax.div(7 * sent, 16))
+    share = lax.shift_right_logical(7 * sent, 4)
     lowest = jnp.where(count > 0, table[T_AGG + W], AD)
 
     def span(agg):
@@ -124,7 +126,7 @@
         return end, floor, even
 
     end, floor, even = lax.fori_loop(lowest, AD, step, (0, 0, 0))
-    split = jnp.maximum(jnp.maximum(end - HALF, floor), jnp.minimum(even, HALF))
+    split = jnp.maximum(jnp.maximum(end - HALF, floor), jnp.minimum(even, EARLY))
     table[T_N] = end
     table[T_H] = split
     if places:
@@ -264,20 +266,20 @@
     return run
 
 
-def clear(acc, begin, end):
-    def step(at, carry):
-        acc[at] = jnp.zeros(acc.shape[1:], acc.dtype)
+def clear_own(acc, begin, end):
+    def step(agg, carry):
+        acc[pl.ds(HALF + 1 + agg * KC, KC)] = jnp.zeros((KC,) + acc.shape[1:], acc.dtype)
         return carry
 
     lax.fori_loop(begin, end, step, 0)
 
 
-def give(acc, out):
+def give(acc, out, amount):
     def step(at, carry):
         out[at] = acc[at].astype(out.dtype)
         return carry
 
-    lax.fori_loop(0, HALF, step, 0)
+    lax.fori_loop(0, amount, step, 0)
 
 
 class Writes:
@@ -350,8 +352,8 @@
         return carry
 
     lax.fori_loop(0, count - ahead, prefetch, 0)
-    scan_rows(pos, devices, rows, begins, table)
-    scan_sent(rows, begins, table, False)
+    scan_rows(pos, devices, rows, begins, table, rows)
+    scan_sent(begins, table, False)
     share_own(rows, begins, table)
     low, own0, own1 = table[T_LO], table[T_OWN0], table[T_OWN1]
     begin = table[T_AGG + own0 + W] - AD
@@ -360,8 +362,8 @@
     run = all_rows(
         ((low, count), (own0, own1)), True, ahead, table[T_H], table[T_N], nbr, cnt, table, blocks, window, applied, turned, items, row_sems, a_hbm, acc, writes
     )
-    clear(acc, 0, HALF)
-    clear(acc, HALF + 1 + begin * KC, HALF + 1 + stop * KC)
+    acc[0:HALF] = jnp.zeros((HALF,) + acc.shape[1:], acc.dtype)
+    clear_own(acc, begin, stop)
     copies[1].wait()
     copies[2].wait()
     copies[3].wait()
@@ -369,7 +371,7 @@
         out[HALF + at] = window[W + at]
         tail[at] = window[rows + at]
     run()
-    give(acc, out)
+    give(acc, out, HALF)
     lax.fori_loop(ahead, low, drain, 0)
     writes.wait()
 
@@ -394,14 +396,14 @@
     run = all_rows(
         ((0, table[T_HI]), (own1, own2)), False, table[T_S], 0, table[T_H], nbr, cnt, table, blocks, window, applied, turned, items, row_sems, a_hbm, acc, writes
     )
-    clear(acc, 0, HALF)
-    clear(acc, HALF + 1 + begin * KC, HALF + 1 + stop * KC)
+    acc[0:HALF] = jnp.zeros((HALF,) + acc.shape[1:], acc.dtype)
+    clear_own(acc, begin, stop)
     copies[2].wait()
     copies[3].wait()
     copies[0].wait()
     copies[1].wait()
     run()
-    give(acc, out)
+    give(acc, out, EARLY)
     writes.wait()
 
 
@@ -426,16 +428,16 @@
     run = all_rows(
         ((count, own0), (own2, rows)), False, count, 0, 0, nbr, cnt, table, blocks, window, applied, turned, items, row_sems, a_hbm, acc, writes
     )
-    clear(acc, HALF + 1, HALF + 1 + skip * KC)
-    clear(acc, HALF + 1 + resume * KC, HALF + 1 + AD * KC)
+    clear_own(acc, 0, skip)
+    clear_own(acc, resume, AD)
     merge[T_N] = 0
     merge[T_H] = 0
 
     @pl.when(pos + 1 < devices)
     def _():
         begins = [table[T_NEXT + at] for at in range(4)]
-        scan_rows(pos + 1, devices, rows, begins, merge)
-        scan_sent(rows, begins, merge, True)
+        scan_rows(pos + 1, devices, rows, begins, merge, SMAX)
+        scan_sent(begins, merge, True)
 
     split = merge[T_H]
 
@@ -540,7 +542,7 @@
     got_late = passed(late, -1)
     early, coarse = pl.pallas_call(
         functools.partial(early_kernel, devices),
-        out_shape=(jax.ShapeDtypeStruct((HALF, width, width), jnp.bfloat16), coarse_shape),
+        out_shape=(jax.ShapeDtypeStruct((EARLY, width, width), jnp.bfloat16), coarse_shape),
         in_specs=[SMEM] + [HBM] * 6,
         out_specs=(VMEM, HBM),
         scratch_shapes=work,
@@ -566,7 +568,7 @@
         out_shape=coarse_shape,
         in_specs=[SMEM, VMEM, VMEM, HBM],
         out_specs=HBM,
-        scratch_shapes=[pltpu.VMEM((HALF, width, width), jnp.float32), DMA((HALF,))],
+        scratch_shapes=[pltpu.VMEM((EARLY, width, width), jnp.float32), DMA((EARLY,))],
         input_output_aliases={3: 0},
         compiler_params=params(32),
         name="merge_rows",

time: 43.5 us -> 53.8 us (1.24)
  the two profiles are of different devices: /device:TPU:25 before, /device:TPU:2 now
where the time goes in v1:
time: 53.8 us; the launch traced here: 54.2 us
  Pallas kernels  35.3 us (66%)
  waiting for transfers between devices  11.8 us (22%)
  starting transfers between devices  6.25 us (12%)
  local copies, waits for them, and re-layouts  0.68 us (1%)
    ppermute x3, waiting for transfers between devices, passed(): lax.ppermute(block, AXES, [(i, i + step) for i in devices if i + step in...  11.8 us
    pallas_call x1, Pallas kernels, shards(): pl.pallas_call(functools.partial(own_kernel, devices), out_shape=(coarse_...  11.6 us
    pallas_call x1, Pallas kernels, shards(): pl.pallas_call(functools.partial(late_kernel, devices), out_shape=(jax.Sh...  11.4 us
    pallas_call x1, Pallas kernels, shards(): pl.pallas_call(functools.partial(early_kernel, devices), out_shape=(jax.S...  10.8 us
    ppermute x3, starting transfers between devices, passed(): lax.ppermute(block, AXES, [(i, i + step) for i in devices if i + step in...  6.25 us
    pallas_call x1, Pallas kernels, shards(): pl.pallas_call(merge_kernel, out_shape=coarse_shape, in_specs=[SMEM, VMEM...  1.46 us
  transfers between devices with their start and end apart: 3, of which 1 were waited for; matrix products, arithmetic and copies ran while one was open for 0% of the time, Pallas kernels for 41%

profile of v1, /device:TPU:2, one launch (start us, length us, event | category | flops | bytes accessed | tf_op | source)
XLA Modules:
  0.0 54.2 jit_solution(1167235168681792091)
XLA Ops:
  0.0 0.0 copy-start
  0.0 0.0 copy-start.1
  0.0 0.0 copy-start.3
  0.0 11.4 %late_rows.1 = (bf16[28,128,128]{2,1,0:T(8,128)(2,1)}, bf16[3,128,128]{2,1,0:T(8,128)(2,1)}, f32[112,128,128]{2,1,0:T(8,128)}, s32[768]{0:T(1024)}) custom-call(s32[32]{0:T(128)} %own_hbm.1, s32[8,64]{1,0:T(8,128)} %bitcast.2, s32[64]{0:T(128)} %cnt_hbm.5, bf16[64,8,128,128]{3,2,1,0:T(8,128)(2,1)} %a_hbm.5, bf16[64,128,128]{2,1,0:T(8,128)(2,1)} %p_hbm.5), custom_call_target="tpu_custom_call" | custom-call | flops 715827904 | bytes 5592405 | tf_op jit(solution)/shard_map/late_rows/pallas_call | solution.py:526
  11.4 1.9 %collective-permute-start.1 = (bf16[28,128,128]{2,1,0:T(8,128)(2,1)}, bf16[28,128,128]{2,1,0:T(8,128)(2,1)S(1)}, u32[]{:S(2)}, u32[]{:S(2)}) collective-permute-start(bf16[28,128,128]{2,1,0:T(8,128)(2,1)} %get-tuple-element.16), channel_id=1, source_target_pairs={{1,0},{2,1},{3,2},{4,3},{5,4},{6,5},{7,6},{8,7},{9,8},{10,9},{11,1... | collective-permute-start | bytes 2752520 | tf_op jit(solution)/shard_map/ppermute | solution.py:501
  13.4 2.4 %collective-permute-start = (bf16[3,128,128]{2,1,0:T(8,128)(2,1)}, bf16[3,128,128]{2,1,0:T(8,128)(2,1)S(1)}, u32[]{:S(2)}, u32[]{:S(2)}) collective-permute-start(bf16[3,128,128]{2,1,0:T(8,128)(2,1)} %get-tuple-element.15), channel_id=1, source_target_pairs={{0,1},{1,2},{2,3},{3,4},{4,5},{5,6},{6,7},{7,8},{8,9},{9,10},{10,1... | collective-permute-start | bytes 294920 | tf_op jit(solution)/shard_map/ppermute | solution.py:501
  15.8 11.8 %collective-permute-done.before = bf16[3,128,128]{2,1,0:T(8,128)(2,1)S(1)} collective-permute-done((bf16[3,128,128]{2,1,0:T(8,128)(2,1)}, bf16[3,128,128]{2,1,0:T(8,128)(2,1)S(1)}, u32[]{:S(2)}, u32[]{:S(2)}) %collective-permute-start) | collective-permute-done | bytes 98336 | tf_op jit(solution)/shard_map/ppermute | solution.py:501
  27.6 0.0 copy-done
  27.6 0.0 copy-done.1
  27.6 0.0 copy-done.3
  27.6 0.0 copy-start.2
  27.6 0.7 %copy-done.2 = s32[768]{0:T(1024)S(1)} copy-done((s32[768]{0:T(1024)S(1)}, s32[768]{0:T(1024)}, u32[]{:S(2)}) %copy-start.2) | copy-done | bytes 3096
  28.3 10.8 %early_rows.1 = (bf16[18,128,128]{2,1,0:T(8,128)(2,1)S(1)}, f32[112,128,128]{2,1,0:T(8,128)}) custom-call(s32[768]{0:T(1024)S(1)} %copy-done.2, s32[8,64]{1,0:T(8,128)S(1)} %bitcast.3, s32[64]{0:T(128)S(1)} %copy-done.3, bf16[64,8,128,128]{3,2,1,0:T(8,128)(2,1)} %a_hbm.5, bf16[64,128,128]{2,1,0:T(8,128)(2,1)S(1)} %copy-done, ...), custom_call_target="tpu_custom_call", output_to_operand_aliasing={{1}: (6, {})} | custom-call | flops 715827904 | bytes 5592405 | tf_op jit(solution)/shard_map/early_rows/pallas_call | solution.py:543
  39.1 1.9 %collective-permute-start.2 = (bf16[18,128,128]{2,1,0:T(8,128)(2,1)S(1)}, bf16[18,128,128]{2,1,0:T(8,128)(2,1)S(1)}, u32[]{:S(2)}, u32[]{:S(2)}) collective-permute-start(bf16[18,128,128]{2,1,0:T(8,128)(2,1)S(1)} %get-tuple-element.20), channel_id=1, source_target_pairs={{1,0},{2,1},{3,2},{4,3},{5,4},{6,5},{7,6},{8,7},{9,8},{10,9},{11,1... | collective-permute-start | bytes 1769480 | tf_op jit(solution)/shard_map/ppermute | solution.py:501
  41.0 0.0 collective-permute-done.1.got
  41.0 11.6 %own_rows.1 = (f32[112,128,128]{2,1,0:T(8,128)}, f32[7,128,128]{2,1,0:T(8,128)S(1)}, s32[768]{0:T(1024)S(1)}) custom-call(s32[768]{0:T(1024)S(1)} %copy-done.2, s32[8,64]{1,0:T(8,128)S(1)} %bitcast.4, s32[64]{0:T(128)S(1)} %copy-done.3, bf16[64,8,128,128]{3,2,1,0:T(8,128)(2,1)} %a_hbm.5, ...), custom_call_target="tpu_custom_call", output_to_operand_aliasing={{0}: (7, {})} | custom-call | flops 715827904 | bytes 5592405 | tf_op jit(solution)/shard_map/own_rows/pallas_call | solution.py:555
  52.7 0.0 collective-permute-done.2.got
  52.7 1.5 %merge_rows.1 = f32[112,128,128]{2,1,0:T(8,128)} custom-call(s32[768]{0:T(1024)S(1)} %get-tuple-element.19.merge, bf16[18,128,128]{2,1,0:T(8,128)(2,1)S(1)} %collective-permute-done.2.got, f32[7,128,128]{2,1,0:T(8,128)S(1)} %get-tuple-element.21.edge, f32[112,128,128]{2,1,0:T(8,128)} %get-tuple-element.22._), custom_call_target="tpu_custom_call", output_to_operand_aliasing={{}: (3, {})} | custom-call | tf_op jit(solution)/shard_map/merge_rows/pallas_call | solution.py:566
Async XLA Ops:
  0.0 27.6 %copy-start = (bf16[64,128,128]{2,1,0:T(8,128)(2,1)S(1)}, bf16[64,128,128]{2,1,0:T(8,128)(2,1)}, u32[]{:S(2)}) copy-start(bf16[64,128,128]{2,1,0:T(8,128)(2,1)} %p_hbm.5) | copy-start | bytes 6291460
  0.0 27.6 %copy-start.1 = (s32[64,8]{0,1:T(8,128)S(1)}, s32[64,8]{0,1:T(8,128)}, u32[]{:S(2)}) copy-start(s32[64,8]{0,1:T(8,128)} %param.6) | copy-start | bytes 6148
  0.0 27.6 %copy-start.3 = (s32[64]{0:T(128)S(1)}, s32[64]{0:T(128)}, u32[]{:S(2)}) copy-start(s32[64]{0:T(128)} %cnt_hbm.5) | copy-start | bytes 772
  11.4 29.6 %collective-permute-start.1 = (bf16[28,128,128]{2,1,0:T(8,128)(2,1)}, bf16[28,128,128]{2,1,0:T(8,128)(2,1)S(1)}, u32[]{:S(2)}, u32[]{:S(2)}) collective-permute-start(bf16[28,128,128]{2,1,0:T(8,128)(2,1)} %get-tuple-element.16), channel_id=1, source_target_pairs={{1,0},{2,1},{3,2},{4,3},{5,4},{6,5},{7,6},{8,7},{9,8},{10,9},{11,1... | collective-permute-start | bytes 2752520 | tf_op jit(solution)/shard_map/ppermute | solution.py:501
  13.4 14.2 %collective-permute-start = (bf16[3,128,128]{2,1,0:T(8,128)(2,1)}, bf16[3,128,128]{2,1,0:T(8,128)(2,1)S(1)}, u32[]{:S(2)}, u32[]{:S(2)}) collective-permute-start(bf16[3,128,128]{2,1,0:T(8,128)(2,1)} %get-tuple-element.15), channel_id=1, source_target_pairs={{0,1},{1,2},{2,3},{3,4},{4,5},{5,6},{6,7},{7,8},{8,9},{9,10},{10,1... | collective-permute-start | bytes 294920 | tf_op jit(solution)/shard_map/ppermute | solution.py:501
  27.6 0.7 %copy-start.2 = (s32[768]{0:T(1024)S(1)}, s32[768]{0:T(1024)}, u32[]{:S(2)}) copy-start(s32[768]{0:T(1024)} %get-tuple-element.14.table) | copy-start | bytes 9220
  39.1 13.6 %collective-permute-start.2 = (bf16[18,128,128]{2,1,0:T(8,128)(2,1)S(1)}, bf16[18,128,128]{2,1,0:T(8,128)(2,1)S(1)}, u32[]{:S(2)}, u32[]{:S(2)}) collective-permute-start(bf16[18,128,128]{2,1,0:T(8,128)(2,1)S(1)} %get-tuple-element.20), channel_id=1, source_target_pairs={{1,0},{2,1},{3,2},{4,3},{5,4},{6,5},{7,6},{8,7},{9,8},{10,9},{11,1... | collective-permute-start | bytes 1769480 | tf_op jit(solution)/shard_map/ppermute | solution.py:501
